TPU v7x, 32 devices: a whole 2x2x4 slice. The times are simulated.
32 devices in a mesh: tm: 8 (over z, x), obs: 4 (over y, core).
Axes of the slice: x: 2, y: 2, z: 4, core: 2. Of those that a mesh axis runs over, the one named last changes fastest.
Arguments:
- observed: float32 [32, 2048], P('tm', 'obs'), may hold values from -6 to 6
- slot_site: int32 [32, 2048], P('tm', 'obs'), may hold values from 0 to 16383
- live_count: int32 [32, 4], P('tm', 'obs'), may hold values from 128 to 512
- site_feature: float32 [16384, 128], replicated, may hold values from -0.5 to 0.5
- site_precision: float32 [16384], replicated, may hold values from 0.5 to 8
- time_scale: float32 [128], replicated, may hold values from 4 to 200
- variance: float32 [128], replicated, may hold values from 0.5 to 2
Outputs:
- filtered_mean: float32 [32, 128], P('tm')
Inputs may be any that keep to these rules, and one draw needn't show every extreme that they name: `slot_site`: slot sites index the sensor locations. `live_count`: live slots of a group come first.
All inputs are finite; a program needn't handle non-finite values.
Results may differ from a plain program's by a relative error of at most 0.0003.
Values sent between devices are 32-bit elements; how exact they have to be, the bound alone decides.
A program may use at most 192 MiB of HBM per device.

v0:
```python
import jax
import jax.numpy as jnp
from jax import lax
from jax.sharding import PartitionSpec as P


def shifted(block, axis, distance):
    devices = range(lax.axis_size(axis))
    route = [(i - distance, i) for i in devices if i - distance in devices]
    return lax.ppermute(block, axis, route)


def matmul_high(left, right):
    return jnp.dot(left, right, precision=lax.Precision.HIGHEST, preferred_element_type=jnp.float32)


def gain_inverse(covariance, precision_mat):
    identity = jnp.eye(covariance.shape[0], dtype=covariance.dtype)
    factor_low = lax.linalg.cholesky(covariance)
    right_side = matmul_high(factor_low.T, precision_mat)
    inner_mat = identity + matmul_high(right_side, factor_low)
    inner_low = lax.linalg.cholesky(inner_mat)
    partial_solve = lax.linalg.triangular_solve(inner_low, right_side, left_side=True, lower=True)
    solved = lax.linalg.triangular_solve(
        inner_low, partial_solve, left_side=True, lower=True, transpose_a=True
    )
    return identity - matmul_high(factor_low, solved)


def combine_full(earlier, later):
    trans_e, mean_e, cov_e, eta_e, prec_e = earlier
    trans_l, mean_l, cov_l, eta_l, prec_l = later
    gain = gain_inverse(cov_e, prec_l)
    moved = matmul_high(trans_l, gain)
    trans_new = matmul_high(moved, trans_e)
    mean_new = matmul_high(moved, mean_e + matmul_high(cov_e, eta_l)) + mean_l
    cov_new = matmul_high(matmul_high(moved, cov_e), trans_l.T) + cov_l
    backward = matmul_high(trans_e.T, gain.T)
    eta_new = matmul_high(backward, eta_l - matmul_high(prec_l, mean_e)) + eta_e
    prec_new = matmul_high(matmul_high(backward, prec_l), trans_e) + prec_e
    return (trans_new, mean_new, cov_new, eta_new, prec_new)


def combine_reduce(prior_mean, prior_cov, later):
    trans_l, mean_l, cov_l, eta_l, prec_l = later
    gain = gain_inverse(prior_cov, prec_l)
    moved = matmul_high(trans_l, gain)
    mean_new = matmul_high(moved, prior_mean + matmul_high(prior_cov, eta_l)) + mean_l
    cov_new = matmul_high(matmul_high(moved, prior_cov), trans_l.T) + cov_l
    return (mean_new, cov_new)


def matern_blocks(time_scale, variance):
    rate = jnp.sqrt(jnp.float32(3.0)) / time_scale
    decay = jnp.exp(-rate)
    twice = 2.0 * rate
    decay_two = jnp.exp(-twice)
    term_now = twice**3 / 6.0
    series = term_now
    for degree in range(4, 17):
        term_now = term_now * twice / degree
        series = series + term_now
    noise_pp = variance * decay_two * series
    noise_pv = 2.0 * rate**3 * decay_two * variance
    noise_vv = rate**2 * variance * decay_two * (jnp.expm1(twice) + twice - 0.5 * twice**2)
    trans = jnp.block(
        [
            [jnp.diag(decay * (1.0 + rate)), jnp.diag(decay)],
            [jnp.diag(-(rate**2) * decay), jnp.diag(decay * (1.0 - rate))],
        ]
    )
    noise = jnp.block(
        [[jnp.diag(noise_pp), jnp.diag(noise_pv)], [jnp.diag(noise_pv), jnp.diag(noise_vv)]]
    )
    station = jnp.diag(jnp.concatenate([variance, rate**2 * variance]))
    return (trans, noise, station)


def step_element(trans_pred, cov_pred, gram_block, info_vec):
    basis_n = gram_block.shape[0]
    states_n = 2 * basis_n
    identity = jnp.eye(states_n, dtype=cov_pred.dtype)
    zero_vec = jnp.zeros((states_n,), cov_pred.dtype)
    zero_mat = jnp.zeros((states_n, states_n), cov_pred.dtype)
    prec_full = jnp.pad(gram_block, ((0, basis_n), (0, basis_n)))
    info_full = jnp.pad(info_vec, ((0, basis_n),))
    predicted = (trans_pred, zero_vec, cov_pred, zero_vec, zero_mat)
    updated = (identity, zero_vec, zero_mat, info_full, prec_full)
    return combine_full(predicted, updated)


def climb_merge(received, holding):

    def merged(both):
        arrived, mine = both
        result = combine_full(arrived[:5], mine[:5])
        return result + (mine[5],)

    def retained(both):
        return both[1]

    return lax.cond(received[5][0] > 0.5, merged, retained, (received, holding))


def body(observed, slot_site, live_count, site_feature, site_precision, time_scale, variance):
    steps_local = observed.shape[0]
    slots_local = observed.shape[1]
    rank_of = jnp.arange(slots_local, dtype=jnp.int32)
    live = (rank_of[None, :] < live_count).astype(jnp.float32)
    weight = site_precision[slot_site] * live
    feature = site_feature[slot_site]
    weighted = feature * weight[:, :, None]
    gram_part = jnp.einsum("tna,tnb->tab", weighted, feature, precision=lax.Precision.HIGHEST)
    info_part = jnp.einsum("tn,tna->ta", observed, weighted, precision=lax.Precision.HIGHEST)
    gram, info = lax.psum((gram_part, info_part), "obs")
    trans, noise, station = matern_blocks(time_scale, variance)
    block_index = lax.axis_index("tm")
    prefixes = []
    for step_now in range(steps_local):
        is_first = jnp.logical_and(block_index == 0, step_now == 0)
        trans_pred = jnp.where(is_first, jnp.zeros_like(trans), trans)
        cov_pred = jnp.where(is_first, station, noise)
        element = step_element(trans_pred, cov_pred, gram[step_now], info[step_now])
        if step_now == 0:
            prefixes.append(element)
        else:
            prefixes.append(combine_full(prefixes[-1], element))
    holding = prefixes[-1] + (jnp.ones((1,), jnp.float32),)
    levels = lax.axis_size("tm").bit_length() - 1
    for level_now in range(levels):
        stride = 1 << level_now
        received = shifted(holding, "tm", stride)
        holding = climb_merge(received, holding)
    before_mean, before_cov, before_flag = shifted((holding[1], holding[2], holding[5]), "tm", 1)

    def joined(inputs):
        prior_mean, prior_cov, local = inputs
        return combine_reduce(prior_mean, prior_cov, local)[0]

    def alone(inputs):
        return inputs[2][1]

    outputs = []
    for step_now in range(steps_local):
        if step_now == steps_local - 1:
            mean_step = holding[1]
        else:
            mean_step = lax.cond(
                before_flag[0] > 0.5, joined, alone, (before_mean, before_cov, prefixes[step_now])
            )
        outputs.append(mean_step[: gram.shape[1]])
    return jnp.stack(outputs, axis=0)


def solution(mesh):
    in_specs = (P("tm", "obs"), P("tm", "obs"), P("tm", "obs"), P(), P(), P(), P())
    out_specs = P("tm", None)
    return jax.shard_map(body, mesh=mesh, in_specs=in_specs, out_specs=out_specs, check_vma=False)
```

profile of v0, /device:TPU:25, one launch (start us, length us, event | category | flops | bytes accessed | tf_op | source)
XLA Modules:
  0.0 1541.7 jit_solution(6405041355622626360)
XLA Ops:
  11.2 11.8 gather_fusion.1
  35.0 11.7 custom-call.165
  57.3 12.0 custom-call.157
  80.5 11.7 custom-call.167
  122.9 11.7 custom-call.160
  145.8 12.1 custom-call.162
  164.0 19.7 %custom-call.164 = f32[2,128,128]{1,2,0:T(8,128)S(1)} custom-call(f32[2,128,128]{2,1,0:T(8,128)S(1)} %get-tuple-element.410), custom_call_target="InvertDiagBlocksLowerTriangular" | custom-call | tf_op jit(solution)/shard_map/triangular_solve/custom-call.4 | solution.py:24
  188.9 11.7 custom-call.183
  211.8 11.9 custom-call.178
  234.8 11.7 custom-call.180
  252.6 19.9 %custom-call.182 = f32[2,128,128]{1,2,0:T(8,128)S(1)} custom-call(f32[2,128,128]{2,1,0:T(8,128)S(1)} %get-tuple-element.416), custom_call_target="InvertDiagBlocksLowerTriangular" | custom-call | tf_op jit(solution)/shard_map/triangular_solve/custom-call.4 | solution.py:24
  294.1 12.1 custom-call.186
  338.3 19.8 %custom-call.190 = f32[2,128,128]{1,2,0:T(8,128)S(1)} custom-call(f32[2,128,128]{2,1,0:T(8,128)S(1)} %get-tuple-element.418), custom_call_target="InvertDiagBlocksLowerTriangular" | custom-call | tf_op jit(solution)/shard_map/triangular_solve/custom-call.4 | solution.py:24
  366.4 11.7 custom-call.191
  391.0 11.9 custom-call.173
  433.3 20.1 %custom-call.177 = f32[2,128,128]{1,2,0:T(8,128)S(1)} custom-call(f32[2,128,128]{2,1,0:T(8,128)S(1)} %get-tuple-element.414), custom_call_target="InvertDiagBlocksLowerTriangular" | custom-call | tf_op jit(solution)/shard_map/triangular_solve/custom-call.4 | solution.py:24
  460.1 12.5 custom-call.193
  484.4 12.7 custom-call.194
  514.5 12.5 custom-call.196
  543.1 21.3 %custom-call.198 = f32[2,128,128]{1,2,0:T(8,128)} custom-call(f32[2,128,128]{2,1,0:T(8,128)} %get-tuple-element.420), custom_call_target="InvertDiagBlocksLowerTriangular" | custom-call | tf_op jit(solution)/shard_map/triangular_solve/custom-call.4 | solution.py:24
  606.6 12.1 custom-call.168
  632.7 12.3 custom-call.170
  657.6 21.2 %custom-call.172 = f32[2,128,128]{1,2,0:T(8,128)} custom-call(f32[2,128,128]{2,1,0:T(8,128)} %get-tuple-element.412), custom_call_target="InvertDiagBlocksLowerTriangular" | custom-call | tf_op jit(solution)/shard_map/triangular_solve/custom-call.4 | solution.py:24
  691.4 13.2 custom-call.201
  717.3 13.4 custom-call.202
  750.3 13.2 custom-call.204
  780.5 21.5 %custom-call.206 = f32[2,128,128]{1,2,0:T(8,128)} custom-call(f32[2,128,128]{2,1,0:T(8,128)} %get-tuple-element.422), custom_call_target="InvertDiagBlocksLowerTriangular" | custom-call | tf_op jit(solution)/shard_map/triangular_solve/custom-call.4 | solution.py:24
  851.4 112.9 %conditional.6 = (f32[256,256]{1,0:T(8,128)S(1)}, f32[256]{0:T(256)S(1)}, f32[256,256]{1,0:T(8,128)S(1)}, f32[256]{0:T(256)S(1)}, f32[256,256]{1,0:T(8,128)S(1)}) conditional(s32[]{:T(128)} %bitcast.120, (f32[256,256]{1,0:T(8,128)S(1)}, f32[256]{0:T(256)S(1)}, f32[256,256]{1,0:T(8,128)S(1)}, f32[256]{0:T(256)S(1)}, ...), branch_computations={%region_6.10_spmd, %region_7.11_spmd} | conditional | flops 2421327360 | bytes 20473168 | solution.py:102
  852.6 11.7 custom-call.109
  874.8 11.7 custom-call.111
  890.4 11.9 custom-call.112
  915.2 11.7 custom-call.114
  934.6 20.5 %custom-call.116 = f32[2,128,128]{1,2,0:T(8,128)S(1)} custom-call(f32[2,128,128]{2,1,0:T(8,128)} %get-tuple-element.398), custom_call_target="InvertDiagBlocksLowerTriangular" | custom-call | tf_op jit(solution)/shard_map/cond/branch_1_fun/triangular_solve/custom-call.4 | solution.py:24
  970.9 12.8 collective-permute-done.2
  988.0 110.7 %conditional.7 = ((f32[256,256]{1,0:T(8,128)S(1)}, f32[256]{0:T(256)S(1)}, f32[256,256]{1,0:T(8,128)S(1)}, f32[256]{0:T(256)S(1)}, f32[256,256]{1,0:T(8,128)S(1)})) conditional(s32[]{:T(128)} %bitcast.145, (f32[256,256]{1,0:T(8,128)S(1)}, f32[256]{0:T(256)S(1)}, f32[256,256]{1,0:T(8,128)S(1)}, f32[256]{0:T(256)S(1)}, ...), branch_computations={%region_8.12_spmd, %region_9.13_spmd} | conditional | flops 2421327360 | bytes 19948860 | solution.py:102
  988.9 11.7 custom-call.117
  1011.1 11.7 custom-call.119
  1026.6 11.9 custom-call.120
  1051.4 11.7 custom-call.122
  1070.7 20.5 %custom-call.124 = f32[2,128,128]{1,2,0:T(8,128)S(1)} custom-call(f32[2,128,128]{2,1,0:T(8,128)} %get-tuple-element.400), custom_call_target="InvertDiagBlocksLowerTriangular" | custom-call | tf_op jit(solution)/shard_map/cond/branch_1_fun/triangular_solve/custom-call.4 | solution.py:24
  1114.9 105.0 %conditional.8 = (f32[256]{0:T(256)S(1)}, f32[256,256]{1,0:T(8,128)S(1)}, f32[1,128]{1,0:T(1,128)S(1)}) conditional(s32[]{:T(128)} %bitcast.144, (f32[256]{0:T(256)S(1)}, f32[256,256]{1,0:T(8,128)S(1)}) %tuple.89, (f32[256,256]{0,1:T(8,128)S(1)}, f32[256,256]{1,0:T(8,128)S(1)}, f32[256,256]{1,0:T(8,128)S(1)}, f32[256]{0:T(256)S(1)}, ...), branch_computations={%region_10.14_spmd, %region_11.15_spmd} | conditional | flops 1614382080 | bytes 13910251 | solution.py:102
  1115.4 11.7 custom-call.125
  1137.7 11.7 custom-call.127
  1152.6 11.9 custom-call.128
  1175.7 11.7 custom-call.130
  1195.1 20.5 %custom-call.132 = f32[2,128,128]{1,2,0:T(8,128)S(1)} custom-call(f32[2,128,128]{2,1,0:T(8,128)} %get-tuple-element.402), custom_call_target="InvertDiagBlocksLowerTriangular" | custom-call | tf_op jit(solution)/shard_map/cond/branch_1_fun/triangular_solve/custom-call.4 | solution.py:24
  1228.7 101.8 %conditional.11 = (f32[1,128]{1,0:T(1,128)S(1)}) conditional(s32[]{:T(128)} %bitcast.120, f32[256]{0:T(256)S(1)} %get-tuple-element.551, (f32[256,256]{0,1:T(8,128)S(1)}, f32[256,256]{1,0:T(8,128)S(1)}, f32[256,256]{1,0:T(8,128)S(1)}, f32[256]{0:T(256)S(1)}, f32[256]{0:T(256)S(1)}, /*index=5*/f32[256]{0:T(256)S(1)}) %tuple.470), branch_computations={%region_16.20_spmd, %region_17.21_spmd} | conditional | flops 1211663360 | bytes 12074211 | solution.py:148
  1229.3 11.7 custom-call.149
  1251.5 11.7 custom-call.151
  1266.4 11.9 custom-call.152
  1289.5 11.7 custom-call.154
  1307.6 19.7 %custom-call.156 = f32[2,128,128]{1,2,0:T(8,128)S(1)} custom-call(f32[2,128,128]{2,1,0:T(8,128)S(1)} %get-tuple-element.408), custom_call_target="InvertDiagBlocksLowerTriangular" | custom-call | tf_op jit(solution)/shard_map/cond/branch_1_fun/triangular_solve/custom-call.4 | solution.py:24
  1330.5 101.8 %conditional.10 = (f32[1,128]{1,0:T(1,128)S(1)}) conditional(s32[]{:T(128)} %bitcast.120, f32[256]{0:T(256)S(1)} %get-tuple-element.553, (f32[256,256]{0,1:T(8,128)S(1)}, f32[256,256]{1,0:T(8,128)S(1)}, f32[256,256]{1,0:T(8,128)S(1)}, f32[256]{0:T(256)S(1)}, f32[256]{0:T(256)S(1)}, /*index=5*/f32[256]{0:T(256)S(1)}) %tuple.92), branch_computations={%region_14.18_spmd, %region_15.19_spmd} | conditional | flops 1211663360 | bytes 12074211 | solution.py:148
  1331.1 11.7 custom-call.141
  1353.3 11.7 custom-call.143
  1368.2 11.9 custom-call.144
  1391.3 11.7 custom-call.146
  1409.5 19.7 %custom-call.148 = f32[2,128,128]{1,2,0:T(8,128)S(1)} custom-call(f32[2,128,128]{2,1,0:T(8,128)S(1)} %get-tuple-element.406), custom_call_target="InvertDiagBlocksLowerTriangular" | custom-call | tf_op jit(solution)/shard_map/cond/branch_1_fun/triangular_solve/custom-call.4 | solution.py:24
  1432.4 101.4 %conditional.9 = (f32[1,128]{1,0:T(1,128)S(1)}) conditional(s32[]{:T(128)} %bitcast.120, f32[256]{0:T(256)S(1)} %bitcast.1029, (f32[256,256]{0,1:T(8,128)S(1)}, f32[256,256]{1,0:T(8,128)S(1)}, f32[256,256]{1,0:T(8,128)S(1)}, f32[256]{0:T(256)S(1)}, f32[256]{0:T(256)S(1)}, /*index=5*/f32[256]{0:T(256)S(1)}) %tuple.472), branch_computations={%region_12.16_spmd, %region_13.17_spmd} | conditional | flops 1211663360 | bytes 12074211 | solution.py:148
  1432.9 11.7 custom-call.133
  1455.2 11.7 custom-call.135
  1469.9 11.9 custom-call.136
  1493.0 11.7 custom-call.138
  1510.8 19.7 %custom-call.140 = f32[2,128,128]{1,2,0:T(8,128)S(1)} custom-call(f32[2,128,128]{2,1,0:T(8,128)S(1)} %get-tuple-element.404), custom_call_target="InvertDiagBlocksLowerTriangular" | custom-call | tf_op jit(solution)/shard_map/cond/branch_1_fun/triangular_solve/custom-call.4 | solution.py:24
  (867 shorter events, 755.2 us)
Async XLA Ops:
  6.5 4.7 copy-start
  6.5 110.5 %all-reduce.11.cloned.1.call-start = ((), (), s32[]{:S(2)}) async-start(), calls=%async_computation | async-start | bytes 524288 | tf_op jit(solution)/shard_map/psum | solution.py:115
  6.5 833.3 %collective-permute-start = (f32[1]{0:T(128)}, f32[1]{0:T(128)}, u32[]{:S(2)}, u32[]{:S(2)}) collective-permute-start(f32[1]{0:T(128)} %constant.145.clone.1), channel_id=1, source_target_pairs={{0,4},{4,8},{8,12},{12,16},{16,20},{20,24},{24,28},{1,5},{5,9},{9,... | collective-permute-start | bytes 20 | tf_op jit(solution)/shard_map/ppermute | solution.py:10
  11.2 21.0 %copy-start.49 = (s32[4,1]{0,1:T(1,128)S(1)}, s32[4,1]{0,1:T(1,128)}, u32[]{:S(2)}) copy-start(s32[4,1]{0,1:T(1,128)} %param.26) | copy-start | bytes 52
  23.0 11.2 copy-start.50
  23.0 11.2 copy-start.48
  23.0 82.3 %copy-start.47 = (f32[4,512]{1,0:T(4,128)S(1)}, f32[4,512]{1,0:T(4,128)}, u32[]{:S(2)}) copy-start(f32[4,512]{1,0:T(4,128)} %param.24) | copy-start | bytes 24580
  34.5 241.5 %copy-start.22 = (f32[128,128]{1,0:T(8,128)}, f32[128,128]{1,0:T(8,128)S(1)}, u32[]{:S(2)}) copy-start(f32[128,128]{1,0:T(8,128)S(1)} %get-tuple-element.727) | copy-start | bytes 196612
  34.5 241.5 %copy-start.24 = (f32[128,128]{1,0:T(8,128)}, f32[128,128]{1,0:T(8,128)S(1)}, u32[]{:S(2)}) copy-start(f32[128,128]{1,0:T(8,128)S(1)} %get-tuple-element.728) | copy-start | bytes 196612
  118.0 3.7 copy-start.28
  118.1 3.7 copy-start.30
  118.1 3.7 copy-start.31
  164.0 19.7 %copy-start.51 = (s32[2,2]{1,0:T(2,128)}, s32[2,2]{1,0:T(2,128)S(1)}, u32[]{:S(2)}) copy-start(s32[2,2]{1,0:T(2,128)S(1)} %get-tuple-element.1386) | copy-start | bytes 52
  185.9 62.8 %copy-start.52 = (s32[2,2]{1,0:T(2,128)S(1)}, s32[2,2]{1,0:T(2,128)}, u32[]{:S(2)}) copy-start(s32[2,2]{1,0:T(2,128)} %copy-done.51) | copy-start | bytes 52
  186.2 24.9 %copy-start.14 = (f32[256,256]{1,0:T(8,128)}, f32[256,256]{1,0:T(8,128)S(1)}, u32[]{:S(2)}) copy-start(f32[256,256]{1,0:T(8,128)S(1)} %fusion.306) | copy-start | bytes 786436
  275.0 88.7 %copy-start.2 = (f32[256,256]{1,0:T(8,128)}, f32[256,256]{1,0:T(8,128)S(1)}, u32[]{:S(2)}) copy-start(f32[256,256]{1,0:T(8,128)S(1)} %fusion.303) | copy-start | bytes 786436
  275.6 88.1 %copy-start.8 = (f32[256,256]{1,0:T(8,128)}, f32[256,256]{1,0:T(8,128)S(1)}, u32[]{:S(2)}) copy-start(f32[256,256]{1,0:T(8,128)S(1)} %fusion.529) | copy-start | bytes 786436
  293.3 0.7 copy-start.34
  455.8 117.8 %copy-start.3 = (f32[256,256]{1,0:T(8,128)}, f32[256,256]{1,0:T(8,128)S(1)}, u32[]{:S(2)}) copy-start(f32[256,256]{1,0:T(8,128)S(1)} %fusion.304) | copy-start | bytes 786436
  456.4 115.0 %copy-start.10 = (f32[256,256]{1,0:T(8,128)}, f32[256,256]{1,0:T(8,128)S(1)}, u32[]{:S(2)}) copy-start(f32[256,256]{1,0:T(8,128)S(1)} %fusion.527) | copy-start | bytes 786436
  478.4 0.7 copy-start.17
  483.1 0.7 copy-start.35
  497.1 1.2 copy-start.43
  571.8 116.2 %copy-start.23 = (f32[128,128]{1,0:T(8,128)S(1)}, f32[128,128]{1,0:T(8,128)}, u32[]{:S(2)}) copy-start(f32[128,128]{1,0:T(8,128)} %copy-done.22) | copy-start | bytes 196612
  605.9 0.7 copy-start.36
  647.6 1.9 copy-start.25
  685.6 22.2 %copy-start.4 = (f32[256,256]{1,0:T(8,128)}, f32[256,256]{1,0:T(8,128)S(1)}, u32[]{:S(2)}) copy-start(f32[256,256]{1,0:T(8,128)S(1)} %fusion.305) | copy-start | bytes 786436
  711.3 0.7 copy-start.16
  716.0 0.7 copy-start.37
  802.0 16.7 %copy-start.15 = (f32[256,256]{1,0:T(8,128)S(1)}, f32[256,256]{1,0:T(8,128)}, u32[]{:S(2)}) copy-start(f32[256,256]{1,0:T(8,128)} %copy-done.14) | copy-start | bytes 786436
  802.0 17.1 %copy-start.13 = (f32[256,256]{1,0:T(8,128)S(1)}, f32[256,256]{1,0:T(8,128)}, u32[]{:S(2)}) copy-start(f32[256,256]{1,0:T(8,128)} %fusion.309) | copy-start | bytes 786436
  802.1 17.1 %copy-start.29 = (f32[128,128]{1,0:T(8,128)S(1)}, f32[128,128]{1,0:T(8,128)}, u32[]{:S(2)}) copy-start(f32[128,128]{1,0:T(8,128)} %copy-done.28) | copy-start | bytes 196612
  802.1 18.2 %copy-start.9 = (f32[256,256]{1,0:T(8,128)S(1)}, f32[256,256]{1,0:T(8,128)}, u32[]{:S(2)}) copy-start(f32[256,256]{1,0:T(8,128)} %copy-done.8) | copy-start | bytes 786436
  802.1 20.4 %copy-start.6 = (f32[256,256]{1,0:T(8,128)S(1)}, f32[256,256]{1,0:T(8,128)}, u32[]{:S(2)}) copy-start(f32[256,256]{1,0:T(8,128)} %fusion.603) | copy-start | bytes 786436
  802.1 21.5 %copy-start.11 = (f32[256,256]{1,0:T(8,128)S(1)}, f32[256,256]{1,0:T(8,128)}, u32[]{:S(2)}) copy-start(f32[256,256]{1,0:T(8,128)} %copy-done.10) | copy-start | bytes 786436
  802.1 23.7 %copy-start.7 = (f32[256,256]{1,0:T(8,128)S(1)}, f32[256,256]{1,0:T(8,128)}, u32[]{:S(2)}) copy-start(f32[256,256]{1,0:T(8,128)} %fusion.600) | copy-start | bytes 786436
  802.1 24.7 %copy-start.12 = (f32[256,256]{1,0:T(8,128)S(1)}, f32[256,256]{1,0:T(8,128)}, u32[]{:S(2)}) copy-start(f32[256,256]{1,0:T(8,128)} %fusion.525) | copy-start | bytes 786436
  803.5 26.2 %copy-start.5 = (f32[256,256]{1,0:T(8,128)S(1)}, f32[256,256]{1,0:T(8,128)}, u32[]{:S(2)}) copy-start(f32[256,256]{1,0:T(8,128)} %fusion.532) | copy-start | bytes 786436
  805.9 26.2 %copy-start.27 = (f32[256,256]{1,0:T(8,128)S(1)}, f32[256,256]{1,0:T(8,128)}, u32[]{:S(2)}) copy-start(f32[256,256]{1,0:T(8,128)} %fusion.520) | copy-start | bytes 786436
  820.3 31.1 %copy-start.18 = (f32[256,256]{1,0:T(8,128)}, f32[256,256]{1,0:T(8,128)S(1)}, u32[]{:S(2)}) copy-start(f32[256,256]{1,0:T(8,128)S(1)} %fusion.307) | copy-start | bytes 786436
  830.2 21.2 %collective-permute-start.4 = (f32[256,256]{1,0:T(8,128)S(1)}, f32[256,256]{1,0:T(8,128)S(1)}, u32[]{:S(2)}, u32[]{:S(2)}) collective-permute-start(f32[256,256]{1,0:T(8,128)S(1)} %fusion.585), channel_id=1, source_target_pairs={{0,4},{4,8},{8,12},{12,16},{16,20},{20,24},{24,28},{1,5},{5,9},{9,... | collective-permute-start | bytes 786440 | tf_op jit(solution)/shard_map/ppermute | solution.py:10
  832.5 18.9 %collective-permute-start.3 = (f32[256,256]{1,0:T(8,128)S(1)}, f32[256,256]{1,0:T(8,128)S(1)}, u32[]{:S(2)}, u32[]{:S(2)}) collective-permute-start(f32[256,256]{1,0:T(8,128)S(1)} %convolution_add_fusion.8), channel_id=1, source_target_pairs={{0,4},{4,8},{8,12},{12,16},{16,20},{20,24},{24,28},{1,5},{5,9},{9,... | collective-permute-start | bytes 786440 | tf_op jit(solution)/shard_map/ppermute | solution.py:10
  835.2 16.2 %copy-start.20 = (f32[256,256]{1,0:T(8,128)}, f32[256,256]{1,0:T(8,128)S(1)}, u32[]{:S(2)}) copy-start(f32[256,256]{1,0:T(8,128)S(1)} %convolution_add_fusion.6) | copy-start | bytes 786436
  835.6 15.8 %collective-permute-start.7 = (f32[256,256]{1,0:T(8,128)S(1)}, f32[256,256]{1,0:T(8,128)S(1)}, u32[]{:S(2)}, u32[]{:S(2)}) collective-permute-start(f32[256,256]{1,0:T(8,128)S(1)} %convolution_add_fusion.7), channel_id=1, source_target_pairs={{0,4},{4,8},{8,12},{12,16},{16,20},{20,24},{24,28},{1,5},{5,9},{9,... | collective-permute-start | bytes 786440 | tf_op jit(solution)/shard_map/ppermute | solution.py:10
  837.5 13.8 collective-permute-start.6
  839.8 11.6 collective-permute-start.5
  851.6 0.8 copy-start.45
  889.7 0.7 copy-start.32
  964.4 23.6 %collective-permute-start.8 = (f32[256,256]{0,1:T(8,128)S(1)}, f32[256,256]{0,1:T(8,128)S(1)}, u32[]{:S(2)}, u32[]{:S(2)}) collective-permute-start(f32[256,256]{0,1:T(8,128)S(1)} %copy.119), channel_id=1, source_target_pairs={{0,8},{4,12},{8,16},{12,20},{16,24},{20,28},{1,9},{5,13},{9,17},{1... | collective-permute-start | bytes 786440 | tf_op jit(solution)/shard_map/ppermute | solution.py:10
  965.7 22.3 %collective-permute-start.12 = (f32[256,256]{1,0:T(8,128)S(1)}, f32[256,256]{1,0:T(8,128)S(1)}, u32[]{:S(2)}, u32[]{:S(2)}) collective-permute-start(f32[256,256]{1,0:T(8,128)S(1)} %get-tuple-element.220), channel_id=1, source_target_pairs={{0,8},{4,12},{8,16},{12,20},{16,24},{20,28},{1,9},{5,13},{9,17},{1... | collective-permute-start | bytes 786440 | tf_op jit(solution)/shard_map/ppermute | solution.py:10
  967.0 21.0 %collective-permute-start.9 = (f32[256,256]{1,0:T(8,128)S(1)}, f32[256,256]{1,0:T(8,128)S(1)}, u32[]{:S(2)}, u32[]{:S(2)}) collective-permute-start(f32[256,256]{1,0:T(8,128)S(1)} %get-tuple-element.221), channel_id=1, source_target_pairs={{0,8},{4,12},{8,16},{12,20},{16,24},{20,28},{1,9},{5,13},{9,17},{1... | collective-permute-start | bytes 786440 | tf_op jit(solution)/shard_map/ppermute | solution.py:10
  968.3 15.4 collective-permute-start.2
  969.6 16.3 %collective-permute-start.11 = (f32[256]{0:T(256)S(1)}, f32[256]{0:T(256)S(1)}, u32[]{:S(2)}, u32[]{:S(2)}) collective-permute-start(f32[256]{0:T(256)S(1)} %get-tuple-element.222), channel_id=1, source_target_pairs={{0,8},{4,12},{8,16},{12,20},{16,24},{20,28},{1,9},{5,13},{9,17},{1... | collective-permute-start | bytes 3080 | tf_op jit(solution)/shard_map/ppermute | solution.py:10
  983.7 4.3 collective-permute-start.10
  988.0 0.7 copy-start.46
  1025.9 0.7 copy-start.33
  1098.7 130.0 %copy-start.21 = (f32[256,256]{1,0:T(8,128)S(1)}, f32[256,256]{1,0:T(8,128)}, u32[]{:S(2)}) copy-start(f32[256,256]{1,0:T(8,128)} %copy-done.20) | copy-start | bytes 786436
  1098.8 16.0 %collective-permute-start.13 = (f32[256,256]{0,1:T(8,128)S(1)}, f32[256,256]{0,1:T(8,128)S(1)}, u32[]{:S(2)}, u32[]{:S(2)}) collective-permute-start(f32[256,256]{0,1:T(8,128)S(1)} %copy.120), channel_id=1, source_target_pairs={{0,16},{4,20},{8,24},{12,28},{1,17},{5,21},{9,25},{13,29},{2,18},{... | collective-permute-start | bytes 786440 | tf_op jit(solution)/shard_map/ppermute | solution.py:10
  1100.1 14.7 collective-permute-start.14
  1101.4 12.7 collective-permute-start.1
  1220.0 8.7 collective-permute-start.15
  1222.0 6.7 collective-permute-start.16
  1330.5 101.8 %copy-start.19 = (f32[256,256]{1,0:T(8,128)S(1)}, f32[256,256]{1,0:T(8,128)}, u32[]{:S(2)}) copy-start(f32[256,256]{1,0:T(8,128)} %copy-done.18) | copy-start | bytes 786436
  1432.3 102.0 %copy-start.1 = (f32[16384]{0:T(1024)S(1)}, f32[16384]{0:T(1024)}, u32[]{:S(2)}) copy-start(f32[16384]{0:T(1024)} %param.28) | copy-start | bytes 196612
  (7 other events, 4.5 us)
Sparse Core Ops, SparseCore 0:
  34.3 32.1 all-reduce.10
where the time goes:
time: 1560 us; the launch traced here: 1540 us
  other arithmetic  1130 us (72%)
  matrix products  155 us (10%)
  local copies, waits for them, and re-layouts  128 us (8%)
  waiting for transfers between devices  40.3 us (3%)
  between operations  33.7 us (2%)
  starting transfers between devices  29.1 us (2%)
  loops' own time  21.1 us (1%)
    another operation x91, other arithmetic, gain_inverse(): inner_low = lax.linalg.cholesky(inner_mat)  469 us
    another operation x71, other arithmetic, gain_inverse(): factor_low = lax.linalg.cholesky(covariance)  383 us
    another operation x39, other arithmetic, gain_inverse(): lax.linalg.triangular_solve(inner_low, partial_solve, left_side=True, low...  269 us
    dot_general x152, matrix products, matmul_high(): jnp.dot(left, right, precision=lax.Precision.HIGHEST, preferred_element_t...  83.2 us
    another operation x92, local copies, waits for them, and re-layouts, gain_inverse(): lax.linalg.triangular_solve(inner_low, partial_solve, left_side=True, low...  71 us
    ppermute x17, waiting for transfers between devices, shifted(): return lax.ppermute(block, axis, route)  40.3 us
  transfers between devices with their start and end apart: 18, of which 6 were waited for; matrix products, arithmetic and copies ran while one was open for 51% of the time, Pallas kernels for 0%

commit v1 on v0

v1 whole, which is shorter than its diff:
```python
import functools

import jax
import jax.numpy as jnp
from jax import lax
from jax.experimental import pallas as pl
from jax.experimental.pallas import tpu as pltpu
from jax.sharding import PartitionSpec as P

F32 = jnp.float32
BF16 = jnp.bfloat16


def dot_full(left, right):
    return jnp.dot(left, right, precision=lax.Precision.HIGHEST, preferred_element_type=F32)


def split(value):
    high = value.astype(BF16)
    return high, (value - high.astype(F32)).astype(BF16)


def dot_three(left, right):
    left_high, left_low = split(left)
    right_high, right_low = split(right)
    sides = jnp.concatenate([left_high, left_low], axis=1)
    tops = jnp.concatenate([right_high, right_high], axis=0)
    first = jnp.dot(sides, tops, preferred_element_type=F32)
    return first + jnp.dot(left_high, right_low, preferred_element_type=F32)


def matern_rows(time_scale, variance):
    rate = jnp.sqrt(F32(3.0)) / time_scale
    decay = jnp.exp(-rate)
    twice = 2.0 * rate
    decay_two = jnp.exp(-twice)
    term_now = twice**3 / 6.0
    series = term_now
    for degree in range(4, 17):
        term_now = term_now * twice / degree
        series = series + term_now
    noise_pp = variance * decay_two * series
    noise_pv = 2.0 * rate**3 * decay_two * variance
    noise_vv = rate**2 * variance * decay_two * (jnp.expm1(twice) + twice - 0.5 * twice**2)
    rows = [
        decay * (1.0 + rate),
        decay,
        -(rate**2) * decay,
        decay * (1.0 - rate),
        noise_pp,
        noise_pv,
        noise_vv,
        variance,
        rate**2 * variance,
    ]
    rows += [jnp.zeros_like(rate)] * (16 - len(rows))
    return jnp.stack(rows)


def filter_kernel(rows_ref, gram_ref, info_ref, mean_ref, coef_ref):
    steps, basis, _ = gram_ref.shape
    row_i = lax.broadcasted_iota(jnp.int32, (basis, basis), 0)
    col_i = lax.broadcasted_iota(jnp.int32, (basis, basis), 1)
    eye = (row_i == col_i).astype(F32)

    def wide(index):
        return jnp.broadcast_to(rows_ref[index : index + 1, :], (basis, basis))

    right = [wide(index) for index in range(4)]
    left = [value.T for value in right]
    pairs = [(0, 0), (0, 1), (1, 1), (0, 2), (1, 2), (0, 3), (1, 3), (2, 2), (2, 3), (3, 3)]
    for place, (one, two) in enumerate(pairs):
        scale = 0.5 if one == two else 1.0
        coef_ref[place] = scale * left[one] * right[two]
    coef_ref[10] = 0.5 * wide(4) * eye
    coef_ref[11] = wide(5) * eye
    coef_ref[12] = 0.5 * wide(6) * eye
    step_a = rows_ref[0:1, :]
    step_b = rows_ref[1:2, :]
    step_c = rows_ref[2:3, :]
    step_d = rows_ref[3:4, :]

    def advance(step, carry):
        cov_pp, cov_pv, cov_vv, mean_p, mean_v = carry
        gram = gram_ref[step]
        info = info_ref[step]
        both = jnp.concatenate([cov_pp, cov_pv], axis=1)
        seen = dot_full(gram, both)
        target = eye + seen[:, :basis].T
        bound = jnp.max(jnp.sum(jnp.abs(target), axis=1))
        scale = 2.0 / (1.0 + bound)
        start = jnp.concatenate([eye - scale * target, scale * eye], axis=0)

        def squaring(state):
            radius, pair = state
            product = dot_three(pair, pair[:basis])
            pair = jnp.concatenate([product[:basis], pair[basis:] + product[basis:]], axis=0)
            return radius * radius, pair

        _, pair = lax.while_loop(lambda s: s[0] > 3e-3, squaring, ((bound - 1.0) * 0.5 * scale, start))

        def polish(state):
            count, _, inverse = state
            rest = eye - dot_full(target, inverse)
            size = jnp.max(jnp.abs(rest))
            return count + 1, size, inverse + dot_full(inverse, rest)

        _, _, gain = lax.while_loop(
            lambda s: jnp.logical_and(s[0] < 12, s[1] > 2e-3),
            polish,
            (jnp.int32(0), F32(1.0), pair[basis:]),
        )
        both = dot_full(gain, both)
        new_pp = both[:, :basis]
        new_pv = both[:, basis:]
        new_vv = cov_vv - dot_full(seen[:, basis:].T, new_pv)
        residual = info - dot_full(mean_p, gram)
        moved = dot_full(residual, both)
        mean_p = mean_p + moved[:, :basis]
        mean_v = mean_v + moved[:, basis:]
        mean_ref[step] = mean_p
        new_vp = new_pv.T
        half_pp = coef_ref[0] * new_pp + coef_ref[1] * new_pv + coef_ref[2] * new_vv + coef_ref[10]
        half_vv = coef_ref[7] * new_pp + coef_ref[8] * new_pv + coef_ref[9] * new_vv + coef_ref[12]
        next_pv = (
            coef_ref[3] * new_pp
            + coef_ref[4] * new_vp
            + coef_ref[5] * new_pv
            + coef_ref[6] * new_vv
            + coef_ref[11]
        )
        return (
            half_pp + half_pp.T,
            next_pv,
            half_vv + half_vv.T,
            step_a * mean_p + step_b * mean_v,
            step_c * mean_p + step_d * mean_v,
        )

    zero_row = jnp.zeros((8, basis), F32)
    first = (wide(7) * eye, jnp.zeros((basis, basis), F32), wide(8) * eye, zero_row, zero_row)
    lax.fori_loop(0, steps, advance, first)


def run_filter(rows, gram, info):
    steps, basis, _ = gram.shape
    return pl.pallas_call(
        filter_kernel,
        out_shape=jax.ShapeDtypeStruct((steps, 8, basis), F32),
        in_specs=[pl.BlockSpec(memory_space=pltpu.VMEM)] * 3,
        out_specs=pl.BlockSpec(memory_space=pltpu.VMEM),
        scratch_shapes=[pltpu.VMEM((13, basis, basis), F32)],
        compiler_params=pltpu.CompilerParams(vmem_limit_bytes=32 * 1024 * 1024),
    )(rows, gram, info)


def body(observed, slot_site, live_count, site_feature, site_precision, time_scale, variance):
    steps_local, slots_local = observed.shape
    basis = site_feature.shape[1]
    rank_of = jnp.arange(slots_local, dtype=jnp.int32)
    live = (rank_of[None, :] < live_count).astype(F32)
    weight = site_precision[slot_site] * live
    feature = site_feature[slot_site]
    weighted = feature * weight[:, :, None]
    sides = jnp.concatenate([feature, jnp.broadcast_to(observed[:, :, None], (steps_local, slots_local, 8))], axis=2)
    part = jnp.einsum("tna,tnb->tab", sides, weighted, precision=lax.Precision.HIGHEST)
    summed = lax.psum(part, "obs")
    every = lax.all_gather(summed, "tm", axis=0, tiled=True)
    means = run_filter(matern_rows(time_scale, variance), every[:, :basis], every[:, basis:])
    block = lax.axis_index("tm")
    return lax.dynamic_slice(means[:, 0, :], (block * steps_local, 0), (steps_local, basis))


def solution(mesh):
    in_specs = (P("tm", "obs"), P("tm", "obs"), P("tm", "obs"), P(), P(), P(), P())
    out_specs = P("tm", None)
    return jax.shard_map(body, mesh=mesh, in_specs=in_specs, out_specs=out_specs, check_vma=False)
```

time: 1560 us -> 236 us (0.15)
  other arithmetic: 1130 us -> 0.86 us
  matrix products: 155 us -> 2.06 us
  Pallas kernels: 0 us -> 108 us
  local copies, waits for them, and re-layouts: 128 us -> 24.4 us
  waiting for transfers between devices: 40.3 us -> 84.3 us
  starting transfers between devices: 29.1 us -> 0.04 us
  loops' own time: 21.1 us -> 0 us
  between operations: 33.7 us -> 13.5 us
    another operation x202 -> x2, other arithmetic: 1120 us -> 0.05 us  [matern_rows(): return jnp.stack(rows)]
    pallas_call x0 -> x1, Pallas kernels: none -> 108 us  [run_filter(): pl.pallas_call(filter_kernel, out_shape=jax.ShapeDtypeStruct((steps, 8, b...]
    another operation x198 -> x4, local copies, waits for them, and re-layouts: 90.9 us -> 0.06 us  [matern_rows(): return jnp.stack(rows)]
    dot_general x154 -> x1, matrix products: 86.1 us -> 2.06 us  [body(): jnp.einsum('tna,tnb->tab', sides, weighted, precision=lax.Precision.HIGHEST)]
    another operation x126 -> x0, matrix products: 68.6 us -> none  [the longest x39 20.9 us: gain_inverse(): lax.linalg.triangular_solve(inner_low, partial_solve, left_side=True, low...]
    all_gather x0 -> x1, waiting for transfers between devices: none -> 52.1 us  [body(): every = lax.all_gather(summed, 'tm', axis=0, tiled=True)]
    ppermute x17 -> x0, waiting for transfers between devices: 40.3 us -> none  [shifted(): return lax.ppermute(block, axis, route)]
    psum x1, waiting for transfers between devices: 0.02 us -> 32.2 us  [body(): summed = lax.psum(part, 'obs')]
  transfers between devices with their start and end apart: 18 -> 2, of which waited for: 6 -> 2; matrix products, arithmetic and copies ran while one was open for 51% -> 0% of each run, Pallas kernels for 0% -> 0%
where the time goes in v1:
time: 236 us; the launch traced here: 233 us
  Pallas kernels  108 us (46%)
  waiting for transfers between devices  84.3 us (36%)
  local copies, waits for them, and re-layouts  24.4 us (10%)
  between operations  13.5 us (6%)
    pallas_call x1, Pallas kernels, run_filter(): pl.pallas_call(filter_kernel, out_shape=jax.ShapeDtypeStruct((steps, 8, b...  108 us
    all_gather x1, waiting for transfers between devices, body(): every = lax.all_gather(summed, 'tm', axis=0, tiled=True)  52.1 us
    psum x1, waiting for transfers between devices, body(): summed = lax.psum(part, 'obs')  32.2 us
    gather x2, local copies, waits for them, and re-layouts, body(): weight = site_precision[slot_site] * live  11.8 us
    gather x2, local copies, waits for them, and re-layouts, body(): feature = site_feature[slot_site]  9.17 us
  transfers between devices with their start and end apart: 2, of which 2 were waited for; matrix products, arithmetic and copies ran while one was open for 0% of the time, Pallas kernels for 0%

profile of v1, /device:TPU:25, one launch (start us, length us, event | category | flops | bytes accessed | tf_op | source)
XLA Modules:
  0.0 233.2 jit_solution(12226030256078459113)
XLA Ops:
  6.5 0.0 copy-start
  6.5 0.0 all-reduce.2.cloned.1.call-start
  6.5 0.7 fusion.6
  7.3 8.8 %gather_fusion = f32[2048,128]{1,0:T(8,128)S(1)} fusion(f32[16384,128]{1,0:T(8,128)} %param.10, s32[2048]{0:T(1024)S(1)} %broadcast_clamp_fusion), kind=kCustom, calls=%fused_computation | custom fusion | bytes 2105344 | tf_op jit(solution)/shard_map/gather | solution.py:163
  16.1 0.3 copy.10
  16.5 0.0 copy-done
  16.5 0.0 copy-start.3
  16.5 0.0 copy-start.1
  16.5 11.8 %gather_fusion.1 = f32[2048]{0:T(1024)S(1)} fusion(f32[16384]{0:T(1024)S(1)} %copy-done, s32[2048]{0:T(1024)S(1)} %broadcast_clamp_fusion), kind=kCustom, calls=%fused_computation.1 | custom fusion | bytes 24576 | tf_op jit(solution)/shard_map/gather | solution.py:162
  28.3 0.0 copy-start.2
  28.3 0.0 copy-start.4
  28.3 0.0 copy-done.3
  28.3 0.1 fusion.7
  28.4 0.0 copy-done.1
  28.4 2.1 fusion
  30.5 0.0 all-reduce.2.cloned.1.call-update
  30.5 0.0 all-gather.2.cloned.1.call-start
  30.6 32.2 %all-reduce.2.cloned.1.call-done = f32[4,136,128]{2,1,0:T(8,128)} async-done(((f32[4,136,128]{2,1,0:T(8,128)}), f32[4,136,128]{2,1,0:T(8,128)}) %all-reduce.2.cloned.1.call-update) | async-done | bytes 278544 | tf_op jit(solution)/shard_map/psum | solution.py:167
  62.7 0.0 all-gather.2.cloned.1.call-update
  62.8 0.0 copy-done.2
  62.8 0.0 copy-done.4
  62.9 0.1 stack.47.rows_ref
  62.9 52.1 %all-gather.2.cloned.1.call-done = f32[32,136,128]{2,1,0:T(8,128)} async-done(((f32[4,136,128]{2,1,0:T(8,128)}), f32[32,136,128]{2,1,0:T(8,128)}) %all-gather.2.cloned.1.call-update) | async-done | bytes 2228240 | tf_op jit(solution)/shard_map/all_gather | solution.py:168
  115.1 1.8 slice.16.gram_ref
  116.9 0.9 slice.17.info_ref
  117.8 108.0 %shard_map.76 = f32[32,8,128]{2,1,0:T(8,128)S(1)} custom-call(f32[16,128]{1,0:T(8,128)S(1)} %stack.47.rows_ref, f32[32,128,128]{2,1,0:T(8,128)S(1)} %slice.16.gram_ref, f32[32,8,128]{2,1,0:T(8,128)S(1)} %slice.17.info_ref), custom_call_target="tpu_custom_call" | custom-call | tf_op jit(solution)/shard_map/pallas_call | solution.py:147
  225.8 0.6 constant_dynamic-slice_fusion
  (10 shorter events, 0.1 us)
Async XLA Ops:
  6.5 9.9 %copy-start = (f32[16384]{0:T(1024)S(1)}, f32[16384]{0:T(1024)}, u32[]{:S(2)}) copy-start(f32[16384]{0:T(1024)} %param.11) | copy-start | bytes 196612
  6.5 56.2 %all-reduce.2.cloned.1.call-start = ((), (), s32[]{:S(2)}) async-start(), calls=%async_computation | async-start | bytes 557056 | tf_op jit(solution)/shard_map/psum | solution.py:167
  16.5 11.9 %copy-start.3 = (s32[4,1]{0,1:T(1,128)S(1)}, s32[4,1]{0,1:T(1,128)}, u32[]{:S(2)}) copy-start(s32[4,1]{0,1:T(1,128)} %param.9) | copy-start | bytes 52
  16.5 11.9 %copy-start.1 = (f32[4,512]{1,0:T(4,128)S(1)}, f32[4,512]{1,0:T(4,128)}, u32[]{:S(2)}) copy-start(f32[4,512]{1,0:T(4,128)} %param.7) | copy-start | bytes 24580
  28.3 34.5 %copy-start.2 = (f32[128]{0:T(128)S(1)}, f32[128]{0:T(128)}, u32[]{:S(2)}) copy-start(f32[128]{0:T(128)} %param.13) | copy-start | bytes 1540
  28.3 34.5 %copy-start.4 = (f32[128]{0:T(128)S(1)}, f32[128]{0:T(128)}, u32[]{:S(2)}) copy-start(f32[128]{0:T(128)} %param.12) | copy-start | bytes 1540
  30.5 84.5 %all-gather.2.cloned.1.call-start = ((), (), s32[]{:S(2)}) async-start(), calls=%async_computation.1 | async-start | bytes 2506752 | tf_op jit(solution)/shard_map/all_gather | solution.py:168
Sparse Core Ops, SparseCore 0:
  30.6 32.0 all-reduce.1
  64.9 50.0 all-gather.1

commit v2 on v1

--- a/solution.py
+++ b/solution.py
@@ -9,6 +9,7 @@
 
 F32 = jnp.float32
 BF16 = jnp.bfloat16
+MESH = pl.DeviceIdType.MESH
 
 
 def dot_full(left, right):
@@ -57,8 +58,8 @@
     return jnp.stack(rows)
 
 
-def filter_kernel(rows_ref, gram_ref, info_ref, mean_ref, coef_ref):
-    steps, basis, _ = gram_ref.shape
+def filter_kernel(rows_ref, every_ref, mean_ref, coef_ref):
+    steps, _, basis = every_ref.shape
     row_i = lax.broadcasted_iota(jnp.int32, (basis, basis), 0)
     col_i = lax.broadcasted_iota(jnp.int32, (basis, basis), 1)
     eye = (row_i == col_i).astype(F32)
@@ -82,10 +83,10 @@
 
     def advance(step, carry):
         cov_pp, cov_pv, cov_vv, mean_p, mean_v = carry
-        gram = gram_ref[step]
-        info = info_ref[step]
+        gram = every_ref[step, :basis, :]
+        info = every_ref[step, basis : basis + 8, :]
         both = jnp.concatenate([cov_pp, cov_pv], axis=1)
-        seen = dot_full(gram, both)
+        seen = dot_three(gram, both)
         target = eye + seen[:, :basis].T
         bound = jnp.max(jnp.sum(jnp.abs(target), axis=1))
         scale = 2.0 / (1.0 + bound)
@@ -101,19 +102,19 @@
 
         def polish(state):
             count, _, inverse = state
-            rest = eye - dot_full(target, inverse)
+            rest = eye - dot_three(target, inverse)
             size = jnp.max(jnp.abs(rest))
-            return count + 1, size, inverse + dot_full(inverse, rest)
+            return count + 1, size, inverse + dot_three(inverse, rest)
 
         _, _, gain = lax.while_loop(
             lambda s: jnp.logical_and(s[0] < 12, s[1] > 2e-3),
             polish,
             (jnp.int32(0), F32(1.0), pair[basis:]),
         )
-        both = dot_full(gain, both)
+        both = dot_three(gain, both)
         new_pp = both[:, :basis]
         new_pv = both[:, basis:]
-        new_vv = cov_vv - dot_full(seen[:, basis:].T, new_pv)
+        new_vv = cov_vv - dot_three(seen[:, basis:].T, new_pv)
         residual = info - dot_full(mean_p, gram)
         moved = dot_full(residual, both)
         mean_p = mean_p + moved[:, :basis]
@@ -142,31 +143,154 @@
     lax.fori_loop(0, steps, advance, first)
 
 
-def run_filter(rows, gram, info):
-    steps, basis, _ = gram.shape
+def gather_kernel(part_ref, all_ref, recv_ref, rs_send, rs_recv, tm_send, tm_recv, ob_send, ob_recv):
+    blocks, groups, chunk, _ = all_ref.shape
+    block = lax.axis_index("tm")
+    group = lax.axis_index("obs")
+
+    def to_block(distance):
+        return {"tm": lax.rem(block + distance, blocks)}
+
+    def to_group(distance):
+        return {"obs": lax.rem(group + distance, groups)}
+
+    barrier = pltpu.get_barrier_semaphore()
+    for distance in range(1, groups):
+        pl.semaphore_signal(barrier, inc=1, device_id=to_group(distance), device_id_type=MESH)
+
+    def greet(distance, carry):
+        pl.semaphore_signal(barrier, inc=1, device_id=to_block(distance), device_id_type=MESH)
+        return carry
+
+    lax.fori_loop(1, blocks, greet, 0)
+    pl.semaphore_wait(barrier, groups + blocks - 2)
+
+    def scatter(distance):
+        peer = lax.rem(group + distance, groups)
+        return pltpu.make_async_remote_copy(
+            src_ref=part_ref.at[peer],
+            dst_ref=recv_ref.at[distance - 1],
+            send_sem=rs_send.at[distance - 1],
+            recv_sem=rs_recv.at[distance - 1],
+            device_id=to_group(distance),
+            device_id_type=MESH,
+        )
+
+    for distance in range(1, groups):
+        scatter(distance).start()
+    total = part_ref[group]
+    for distance in range(1, groups):
+        scatter(distance).wait_recv()
+        total = total + recv_ref[distance - 1]
+    all_ref[block, group] = total
+
+    def along(distance, source):
+        return pltpu.make_async_remote_copy(
+            src_ref=all_ref.at[source, group],
+            dst_ref=all_ref.at[source, group],
+            send_sem=tm_send.at[distance],
+            recv_sem=tm_recv.at[distance],
+            device_id=to_block(distance),
+            device_id_type=MESH,
+        )
+
+    def across(distance, source, step, owner):
+        return pltpu.make_async_remote_copy(
+            src_ref=all_ref.at[source, owner],
+            dst_ref=all_ref.at[source, owner],
+            send_sem=ob_send.at[distance, step - 1],
+            recv_sem=ob_recv.at[distance, step - 1],
+            device_id=to_group(step),
+            device_id_type=MESH,
+        )
+
+    def send_along(distance, carry):
+        along(distance, block).start()
+        return carry
+
+    lax.fori_loop(1, blocks, send_along, 0)
+    for step in range(1, groups):
+        across(0, block, step, group).start()
+
+    def relay(distance, carry):
+        source = lax.rem(block - distance + blocks, blocks)
+        along(distance, source).wait_recv()
+        for step in range(1, groups):
+            across(distance, source, step, group).start()
+        return carry
+
+    lax.fori_loop(1, blocks, relay, 0)
+
+    def finish(distance, carry):
+        source = lax.rem(block - distance + blocks, blocks)
+        for step in range(1, groups):
+            owner = lax.rem(group - step + groups, groups)
+            across(distance, source, step, owner).wait_recv()
+            across(distance, source, step, group).wait_send()
+        return carry
+
+    lax.fori_loop(0, blocks, finish, 0)
+
+    def sent(distance, carry):
+        along(distance, block).wait_send()
+        return carry
+
+    lax.fori_loop(1, blocks, sent, 0)
+    for distance in range(1, groups):
+        scatter(distance).wait_send()
+
+
+def run_gather(part, blocks):
+    groups, chunk, basis = part.shape
+    dma = pltpu.SemaphoreType.DMA
+    return pl.pallas_call(
+        gather_kernel,
+        out_shape=jax.ShapeDtypeStruct((blocks, groups, chunk, basis), F32),
+        in_specs=[pl.BlockSpec(memory_space=pltpu.VMEM)],
+        out_specs=pl.BlockSpec(memory_space=pltpu.VMEM),
+        scratch_shapes=[
+            pltpu.VMEM((groups - 1, chunk, basis), F32),
+            dma((groups - 1,)),
+            dma((groups - 1,)),
+            dma((blocks,)),
+            dma((blocks,)),
+            dma((blocks, groups - 1)),
+            dma((blocks, groups - 1)),
+        ],
+        compiler_params=pltpu.CompilerParams(
+            collective_id=0, has_side_effects=True, vmem_limit_bytes=32 * 1024 * 1024
+        ),
+    )(part)
+
+
+def run_filter(rows, every):
+    steps, _, basis = every.shape
     return pl.pallas_call(
         filter_kernel,
         out_shape=jax.ShapeDtypeStruct((steps, 8, basis), F32),
-        in_specs=[pl.BlockSpec(memory_space=pltpu.VMEM)] * 3,
+        in_specs=[pl.BlockSpec(memory_space=pltpu.VMEM)] * 2,
         out_specs=pl.BlockSpec(memory_space=pltpu.VMEM),
         scratch_shapes=[pltpu.VMEM((13, basis, basis), F32)],
         compiler_params=pltpu.CompilerParams(vmem_limit_bytes=32 * 1024 * 1024),
-    )(rows, gram, info)
+    )(rows, every)
 
 
 def body(observed, slot_site, live_count, site_feature, site_precision, time_scale, variance):
     steps_local, slots_local = observed.shape
     basis = site_feature.shape[1]
+    blocks, groups = lax.axis_size("tm"), lax.axis_size("obs")
     rank_of = jnp.arange(slots_local, dtype=jnp.int32)
     live = (rank_of[None, :] < live_count).astype(F32)
     weight = site_precision[slot_site] * live
     feature = site_feature[slot_site]
     weighted = feature * weight[:, :, None]
-    sides = jnp.concatenate([feature, jnp.broadcast_to(observed[:, :, None], (steps_local, slots_local, 8))], axis=2)
+    values = jnp.broadcast_to(observed[:, :, None], (steps_local, slots_local, 16))
+    sides = jnp.concatenate([feature, values], axis=2)
     part = jnp.einsum("tna,tnb->tab", sides, weighted, precision=lax.Precision.HIGHEST)
-    summed = lax.psum(part, "obs")
-    every = lax.all_gather(summed, "tm", axis=0, tiled=True)
-    means = run_filter(matern_rows(time_scale, variance), every[:, :basis], every[:, basis:])
+    height = basis + 16
+    every = run_gather(part.reshape(groups, steps_local * height // groups, basis), blocks)
+    every = every.reshape(blocks * steps_local, height, basis)
+    means = run_filter(matern_rows(time_scale, variance), every)
     block = lax.axis_index("tm")
     return lax.dynamic_slice(means[:, 0, :], (block * steps_local, 0), (steps_local, basis))
 

time: 236 us -> 166 us (0.70); the launches traced: 233 us -> 166 us
  waiting for transfers between devices: 84.3 us -> 0 us
  Pallas kernels: 108 us -> 140 us
  between operations: 13.5 us -> 0.11 us
    all_gather x1 -> x0, waiting for transfers between devices: 52.1 us -> none  [body(): every = lax.all_gather(summed, 'tm', axis=0, tiled=True)]
    pallas_call x0 -> x1, Pallas kernels: none -> 38.6 us  [run_gather(): pl.pallas_call(gather_kernel, out_shape=jax.ShapeDtypeStruct((blocks, gro...]
    psum x1 -> x0, waiting for transfers between devices: 32.2 us -> none  [body(): summed = lax.psum(part, 'obs')]
    pallas_call x1, Pallas kernels: 108 us -> 102 us  [run_filter(): pl.pallas_call(filter_kernel, out_shape=jax.ShapeDtypeStruct((steps, 8, b...]
    slice x2 -> x0, local copies, waits for them, and re-layouts: 2.73 us -> none  [the longest x1 1.81 us: body(): every[:, :basis]]
  transfers between devices with their start and end apart: 2 -> 0, of which waited for: 2 -> 0; matrix products, arithmetic and copies ran while one was open for 0% -> 0% of each run, Pallas kernels for 0% -> 0%
where the time goes in v2:
time: 166 us
  Pallas kernels  140 us (84%)
  local copies, waits for them, and re-layouts  22.3 us (13%)
  other arithmetic  2.18 us (1%)
    pallas_call x1, Pallas kernels, run_filter(): pl.pallas_call(filter_kernel, out_shape=jax.ShapeDtypeStruct((steps, 8, b...  102 us
    pallas_call x1, Pallas kernels, run_gather(): pl.pallas_call(gather_kernel, out_shape=jax.ShapeDtypeStruct((blocks, gro...  38.6 us
    gather x2, local copies, waits for them, and re-layouts, body(): weight = site_precision[slot_site] * live  11.8 us
    gather x2, local copies, waits for them, and re-layouts, body(): feature = site_feature[slot_site]  9.17 us

profile of v2, /device:TPU:25, one launch (start us, length us, event | category | flops | bytes accessed | tf_op | source)
XLA Modules:
  0.0 166.3 jit_solution(11018748758415878611)
XLA Ops:
  0.0 0.0 copy-start
  0.0 0.7 fusion.13
  0.7 0.7 fusion.11
  1.4 0.7 stack.47.rows_ref
  2.1 0.7 fusion.6
  2.8 8.8 %gather_fusion = f32[2048,128]{1,0:T(8,128)S(1)} fusion(f32[16384,128]{1,0:T(8,128)} %param.10, s32[2048]{0:T(1024)S(1)} %broadcast_clamp_fusion), kind=kCustom, calls=%fused_computation | custom fusion | bytes 2105344 | tf_op jit(solution)/shard_map/gather | solution.py:285
  11.7 0.3 copy.9
  12.0 0.0 copy-done
  12.0 0.0 copy-start.2
  12.1 0.0 copy-start.1
  12.1 11.8 %gather_fusion.1 = f32[2048]{0:T(1024)S(1)} fusion(f32[16384]{0:T(1024)S(1)} %copy-done, s32[2048]{0:T(1024)S(1)} %broadcast_clamp_fusion), kind=kCustom, calls=%fused_computation.1 | custom fusion | bytes 24576 | tf_op jit(solution)/shard_map/gather | solution.py:284
  23.9 0.0 copy-done.2
  23.9 0.1 fusion.7
  24.0 0.0 copy-done.1
  24.0 1.4 fusion.part_ref
  25.4 38.6 %shard_map.76 = f32[8,4,144,128]{3,2,1,0:T(8,128)S(1)} custom-call(f32[4,144,128]{2,1,0:T(8,128)S(1)} %fusion.part_ref), custom_call_target="tpu_custom_call" | custom-call | tf_op jit(solution)/shard_map/pallas_call | solution.py:246
  64.0 101.7 %shard_map.77 = f32[32,8,128]{2,1,0:T(8,128)S(1)} custom-call(f32[16,128]{1,0:T(8,128)S(1)} %stack.47.rows_ref, f32[32,144,128]{2,1,0:T(8,128)S(1)} %bitcast.24), custom_call_target="tpu_custom_call" | custom-call | tf_op jit(solution)/shard_map/pallas_call | solution.py:268
  165.7 0.6 constant_dynamic-slice_fusion
  (8 shorter events, 0.1 us)
Async XLA Ops:
  0.0 12.0 %copy-start = (f32[16384]{0:T(1024)S(1)}, f32[16384]{0:T(1024)}, u32[]{:S(2)}) copy-start(f32[16384]{0:T(1024)} %param.11) | copy-start | bytes 196612
  12.0 11.8 %copy-start.2 = (s32[4,1]{0,1:T(1,128)S(1)}, s32[4,1]{0,1:T(1,128)}, u32[]{:S(2)}) copy-start(s32[4,1]{0,1:T(1,128)} %param.9) | copy-start | bytes 52
  12.1 11.9 %copy-start.1 = (f32[4,512]{1,0:T(4,128)S(1)}, f32[4,512]{1,0:T(4,128)}, u32[]{:S(2)}) copy-start(f32[4,512]{1,0:T(4,128)} %param.7) | copy-start | bytes 24580

commit v3 on v2

--- a/solution.py
+++ b/solution.py
@@ -143,7 +143,7 @@
     lax.fori_loop(0, steps, advance, first)
 
 
-def gather_kernel(part_ref, all_ref, recv_ref, rs_send, rs_recv, tm_send, tm_recv, ob_send, ob_recv):
+def gather_kernel(part_ref, all_ref, recv_ref, rs_send, rs_recv, tm_send, tm_recv, ob_send, ob_recv, side_send, side_recv):
     blocks, groups, chunk, _ = all_ref.shape
     block = lax.axis_index("tm")
     group = lax.axis_index("obs")
@@ -194,13 +194,29 @@
             device_id_type=MESH,
         )
 
+    pairs = groups // 2
+    sibling = group + 1 - 2 * lax.rem(group, 2)
+
+    def owner_of(member, step):
+        return lax.rem(member - 2 * step + groups, groups)
+
     def across(distance, source, step, owner):
         return pltpu.make_async_remote_copy(
             src_ref=all_ref.at[source, owner],
             dst_ref=all_ref.at[source, owner],
-            send_sem=ob_send.at[distance, step - 1],
-            recv_sem=ob_recv.at[distance, step - 1],
-            device_id=to_group(step),
+            send_sem=ob_send.at[distance, step],
+            recv_sem=ob_recv.at[distance, step],
+            device_id=to_group(2 * step),
+            device_id_type=MESH,
+        )
+
+    def aside(distance, source, step, owner):
+        return pltpu.make_async_remote_copy(
+            src_ref=all_ref.at[source, owner],
+            dst_ref=all_ref.at[source, owner],
+            send_sem=side_send.at[distance, step],
+            recv_sem=side_recv.at[distance, step],
+            device_id={"obs": sibling},
             device_id_type=MESH,
         )
 
@@ -208,24 +224,40 @@
         along(distance, block).start()
         return carry
 
+    def origin(distance):
+        return lax.rem(block - distance + blocks, blocks)
+
+    def share(distance):
+        source = origin(distance)
+        for step in range(1, pairs):
+            across(distance, source, step, group).start()
+        aside(distance, source, 0, group).start()
+
+    def forward(distance):
+        source = origin(distance)
+        for step in range(1, pairs):
+            owner = owner_of(group, step)
+            across(distance, source, step, owner).wait_recv()
+            aside(distance, source, step, owner).start()
+
     lax.fori_loop(1, blocks, send_along, 0)
-    for step in range(1, groups):
-        across(0, block, step, group).start()
+    share(0)
 
     def relay(distance, carry):
-        source = lax.rem(block - distance + blocks, blocks)
-        along(distance, source).wait_recv()
-        for step in range(1, groups):
-            across(distance, source, step, group).start()
+        along(distance, origin(distance)).wait_recv()
+        share(distance)
+        forward(distance - 1)
         return carry
 
     lax.fori_loop(1, blocks, relay, 0)
+    forward(blocks - 1)
 
     def finish(distance, carry):
-        source = lax.rem(block - distance + blocks, blocks)
-        for step in range(1, groups):
-            owner = lax.rem(group - step + groups, groups)
-            across(distance, source, step, owner).wait_recv()
+        source = origin(distance)
+        for step in range(pairs):
+            aside(distance, source, step, owner_of(sibling, step)).wait_recv()
+            aside(distance, source, step, owner_of(group, step)).wait_send()
+        for step in range(1, pairs):
             across(distance, source, step, group).wait_send()
         return carry
 
@@ -254,8 +286,10 @@
             dma((groups - 1,)),
             dma((blocks,)),
             dma((blocks,)),
-            dma((blocks, groups - 1)),
-            dma((blocks, groups - 1)),
+            dma((blocks, groups // 2)),
+            dma((blocks, groups // 2)),
+            dma((blocks, groups // 2)),
+            dma((blocks, groups // 2)),
         ],
         compiler_params=pltpu.CompilerParams(
             collective_id=0, has_side_effects=True, vmem_limit_bytes=32 * 1024 * 1024
@@ -281,7 +315,11 @@
     blocks, groups = lax.axis_size("tm"), lax.axis_size("obs")
     rank_of = jnp.arange(slots_local, dtype=jnp.int32)
     live = (rank_of[None, :] < live_count).astype(F32)
-    weight = site_precision[slot_site] * live
+    table = site_precision.reshape(-1, 128)
+    line = (slot_site[:, :, None] // 128 == jnp.arange(table.shape[0], dtype=jnp.int32)).astype(F32)
+    lane = slot_site[:, :, None] % 128 == jnp.arange(128, dtype=jnp.int32)
+    rows = jnp.einsum("tns,sl->tnl", line, table, precision=lax.Precision.HIGHEST)
+    weight = jnp.sum(jnp.where(lane, rows, 0.0), axis=2) * live
     feature = site_feature[slot_site]
     weighted = feature * weight[:, :, None]
     values = jnp.broadcast_to(observed[:, :, None], (steps_local, slots_local, 16))

time: 166 us -> 149 us (0.90)
  local copies, waits for them, and re-layouts: 22.3 us -> 10.9 us
  Pallas kernels: 140 us -> 134 us
    gather x2 -> x0, local copies, waits for them, and re-layouts: 11.8 us -> none  [body(): weight = site_precision[slot_site] * live]
    pallas_call x1, Pallas kernels: 38.6 us -> 34 us  [run_gather(): pl.pallas_call(gather_kernel, out_shape=jax.ShapeDtypeStruct((blocks, gro...]
    pallas_call x1, Pallas kernels: 102 us -> 99.6 us  [run_filter(): pl.pallas_call(filter_kernel, out_shape=jax.ShapeDtypeStruct((steps, 8, b...]
where the time goes in v3:
time: 149 us
  Pallas kernels  134 us (90%)
  local copies, waits for them, and re-layouts  10.9 us (7%)
  matrix products  2.64 us (2%)
  other arithmetic  2.2 us (1%)
    pallas_call x1, Pallas kernels, run_filter(): pl.pallas_call(filter_kernel, out_shape=jax.ShapeDtypeStruct((steps, 8, b...  99.6 us
    pallas_call x1, Pallas kernels, run_gather(): pl.pallas_call(gather_kernel, out_shape=jax.ShapeDtypeStruct((blocks, gro...  34 us
    gather x2, local copies, waits for them, and re-layouts, body(): feature = site_feature[slot_site]  9.18 us

profile of v3, /device:TPU:25, one launch (start us, length us, event | category | flops | bytes accessed | tf_op | source)
XLA Modules:
  0.0 149.5 jit_solution(14348138918110830683)
XLA Ops:
  0.0 0.0 copy-start
  0.0 0.0 copy-start.2
  0.0 0.7 fusion.17
  0.7 0.7 fusion.15
  1.4 0.7 stack.47.rows_ref
  2.1 0.7 add_select_fusion.1
  2.9 0.0 copy-done
  2.9 1.2 fusion
  4.1 0.0 copy-done.2
  4.1 0.1 fusion.10
  4.2 8.8 %gather_fusion = f32[2048,128]{1,0:T(8,128)S(1)} fusion(f32[16384,128]{1,0:T(8,128)} %param.10, s32[2048]{0:T(1024)S(1)} %broadcast_clamp_fusion), kind=kCustom, calls=%fused_computation | custom fusion | bytes 2105344 | tf_op jit(solution)/shard_map/gather | solution.py:323
  13.0 0.0 copy-start.1
  13.1 0.3 copy.12
  13.4 0.3 copy-done.1
  13.8 1.4 fusion.1.part_ref
  15.2 34.0 %shard_map.76 = f32[8,4,144,128]{3,2,1,0:T(8,128)S(1)} custom-call(f32[4,144,128]{2,1,0:T(8,128)S(1)} %fusion.1.part_ref), custom_call_target="tpu_custom_call" | custom-call | tf_op jit(solution)/shard_map/pallas_call | solution.py:278
  49.2 99.6 %shard_map.77 = f32[32,8,128]{2,1,0:T(8,128)S(1)} custom-call(f32[16,128]{1,0:T(8,128)S(1)} %stack.47.rows_ref, f32[32,144,128]{2,1,0:T(8,128)S(1)} %bitcast.29), custom_call_target="tpu_custom_call" | custom-call | tf_op jit(solution)/shard_map/pallas_call | solution.py:302
  148.9 0.6 constant_dynamic-slice_fusion
  (7 shorter events, 0.0 us)
Async XLA Ops:
  0.0 2.9 %copy-start = (f32[16384]{0:T(1024)S(1)}, f32[16384]{0:T(1024)}, u32[]{:S(2)}) copy-start(f32[16384]{0:T(1024)} %param.11) | copy-start | bytes 196612
  0.0 4.1 %copy-start.2 = (s32[4,1]{0,1:T(1,128)S(1)}, s32[4,1]{0,1:T(1,128)}, u32[]{:S(2)}) copy-start(s32[4,1]{0,1:T(1,128)} %param.9) | copy-start | bytes 52
  13.0 0.7 copy-start.1

commit v4 on v3

--- a/solution.py
+++ b/solution.py
@@ -76,19 +76,21 @@
     coef_ref[10] = 0.5 * wide(4) * eye
     coef_ref[11] = wide(5) * eye
     coef_ref[12] = 0.5 * wide(6) * eye
+    for place, (one, two) in enumerate(pairs[3:7]):
+        coef_ref[13 + place] = left[two] * right[one]
     step_a = rows_ref[0:1, :]
     step_b = rows_ref[1:2, :]
     step_c = rows_ref[2:3, :]
     step_d = rows_ref[3:4, :]
 
     def advance(step, carry):
-        cov_pp, cov_pv, cov_vv, mean_p, mean_v = carry
+        cov_pp, cov_pv, cov_vp, cov_vv, mean_p, mean_v = carry
         gram = every_ref[step, :basis, :]
         info = every_ref[step, basis : basis + 8, :]
         both = jnp.concatenate([cov_pp, cov_pv], axis=1)
-        seen = dot_three(gram, both)
-        target = eye + seen[:, :basis].T
-        bound = jnp.max(jnp.sum(jnp.abs(target), axis=1))
+        seen = dot_three(jnp.concatenate([cov_pp, cov_vp], axis=0), gram)
+        target = eye + seen[:basis]
+        bound = jnp.max(jnp.sum(jnp.abs(target), axis=0))
         scale = 2.0 / (1.0 + bound)
         start = jnp.concatenate([eye - scale * target, scale * eye], axis=0)
 
@@ -114,7 +116,7 @@
         both = dot_three(gain, both)
         new_pp = both[:, :basis]
         new_pv = both[:, basis:]
-        new_vv = cov_vv - dot_three(seen[:, basis:].T, new_pv)
+        new_vv = cov_vv - dot_three(seen[basis:], new_pv)
         residual = info - dot_full(mean_p, gram)
         moved = dot_full(residual, both)
         mean_p = mean_p + moved[:, :basis]
@@ -130,16 +132,25 @@
             + coef_ref[6] * new_vv
             + coef_ref[11]
         )
+        next_vp = (
+            coef_ref[13] * new_pp
+            + coef_ref[14] * new_pv
+            + coef_ref[15] * new_vp
+            + coef_ref[16] * new_vv
+            + coef_ref[11]
+        )
         return (
             half_pp + half_pp.T,
             next_pv,
+            next_vp,
             half_vv + half_vv.T,
             step_a * mean_p + step_b * mean_v,
             step_c * mean_p + step_d * mean_v,
         )
 
     zero_row = jnp.zeros((8, basis), F32)
-    first = (wide(7) * eye, jnp.zeros((basis, basis), F32), wide(8) * eye, zero_row, zero_row)
+    zero_mat = jnp.zeros((basis, basis), F32)
+    first = (wide(7) * eye, zero_mat, zero_mat, wide(8) * eye, zero_row, zero_row)
     lax.fori_loop(0, steps, advance, first)
 
 
@@ -304,7 +315,7 @@
         out_shape=jax.ShapeDtypeStruct((steps, 8, basis), F32),
         in_specs=[pl.BlockSpec(memory_space=pltpu.VMEM)] * 2,
         out_specs=pl.BlockSpec(memory_space=pltpu.VMEM),
-        scratch_shapes=[pltpu.VMEM((13, basis, basis), F32)],
+        scratch_shapes=[pltpu.VMEM((17, basis, basis), F32)],
         compiler_params=pltpu.CompilerParams(vmem_limit_bytes=32 * 1024 * 1024),
     )(rows, every)
 

time: 149 us -> 139 us (0.933); the launches traced: 149 us -> 137 us
  Pallas kernels: 134 us -> 121 us
    pallas_call x1, Pallas kernels: 99.6 us -> 86.8 us  [run_filter(): pl.pallas_call(filter_kernel, out_shape=jax.ShapeDtypeStruct((steps, 8, b...]
where the time goes in v4:
time: 139 us; the launch traced here: 137 us
  Pallas kernels  121 us (87%)
  local copies, waits for them, and re-layouts  10.9 us (8%)
  matrix products  2.64 us (2%)
  other arithmetic  2.2 us (2%)
    pallas_call x1, Pallas kernels, run_filter(): pl.pallas_call(filter_kernel, out_shape=jax.ShapeDtypeStruct((steps, 8, b...  86.8 us
    pallas_call x1, Pallas kernels, run_gather(): pl.pallas_call(gather_kernel, out_shape=jax.ShapeDtypeStruct((blocks, gro...  34 us
    gather x2, local copies, waits for them, and re-layouts, body(): feature = site_feature[slot_site]  9.17 us

profile of v4, /device:TPU:25, one launch (start us, length us, event | category | flops | bytes accessed | tf_op | source)
XLA Modules:
  0.0 136.6 jit_solution(7260927109175883611)
XLA Ops:
  0.0 0.0 copy-start
  0.0 0.0 copy-start.2
  0.0 0.7 fusion.17
  0.7 0.7 fusion.15
  1.4 0.7 stack.47.rows_ref
  2.1 0.7 add_select_fusion.1
  2.9 0.0 copy-done
  2.9 1.2 fusion
  4.1 0.0 copy-done.2
  4.1 0.1 fusion.10
  4.2 8.8 %gather_fusion = f32[2048,128]{1,0:T(8,128)S(1)} fusion(f32[16384,128]{1,0:T(8,128)} %param.10, s32[2048]{0:T(1024)S(1)} %broadcast_clamp_fusion), kind=kCustom, calls=%fused_computation | custom fusion | bytes 2105344 | tf_op jit(solution)/shard_map/gather | solution.py:334
  13.0 0.0 copy-start.1
  13.1 0.3 copy.12
  13.4 0.3 copy-done.1
  13.8 1.4 %fusion.1.part_ref = f32[4,144,128]{2,1,0:T(8,128)S(1)} fusion(f32[4,512,16]{1,2,0:T(8,128)S(1)} %broadcast_in_dim.9, f32[4,512,128]{1,2,0:T(8,128)S(1)} %copy.12, f32[4,512,128]{2,1,0:T(8,128)S(1)} %bitcast.31, f32[4,512]{1,0:T(4,128)S(1)} %fusion.10), kind=kOutput, calls=%fused_computation.3 | convolution fusion | flops 453541888 | bytes 2531328 | tf_op jit(solution)/shard_map/tna,tnb->tab/dot_general | solution.py:338
  15.2 34.0 %shard_map.76 = f32[8,4,144,128]{3,2,1,0:T(8,128)S(1)} custom-call(f32[4,144,128]{2,1,0:T(8,128)S(1)} %fusion.1.part_ref), custom_call_target="tpu_custom_call" | custom-call | tf_op jit(solution)/shard_map/pallas_call | solution.py:289
  49.2 86.8 %shard_map.77 = f32[32,8,128]{2,1,0:T(8,128)S(1)} custom-call(f32[16,128]{1,0:T(8,128)S(1)} %stack.47.rows_ref, f32[32,144,128]{2,1,0:T(8,128)S(1)} %bitcast.29), custom_call_target="tpu_custom_call" | custom-call | tf_op jit(solution)/shard_map/pallas_call | solution.py:313
  136.0 0.6 constant_dynamic-slice_fusion
  (7 shorter events, 0.0 us)
Async XLA Ops:
  0.0 2.9 %copy-start = (f32[16384]{0:T(1024)S(1)}, f32[16384]{0:T(1024)}, u32[]{:S(2)}) copy-start(f32[16384]{0:T(1024)} %param.11) | copy-start | bytes 196612
  0.0 4.1 %copy-start.2 = (s32[4,1]{0,1:T(1,128)S(1)}, s32[4,1]{0,1:T(1,128)}, u32[]{:S(2)}) copy-start(s32[4,1]{0,1:T(1,128)} %param.9) | copy-start | bytes 52
  13.0 0.7 copy-start.1
